TPU v7x, 256 devices: a whole 4x4x8 slice. The times are simulated.
256 devices in a mesh: grp: 2 (over core), gx: 16 (over z_hi, y), gy: 8 (over x, z_lo).
Axes of the slice: x: 4, y: 4, z: 8 (z_hi: 4, z_lo: 2; z = z_hi * 2 + z_lo), core: 2. Of those that a mesh axis runs over, the one named last changes fastest.
Arguments:
- source: bfloat16 [4, 128, 256, 1024], P(None, None, ('grp', 'gx'), 'gy'), may hold values from -6 to 6
- speed: bfloat16 [128, 256, 1024], P(('grp', 'gx'), None, 'gy'), may hold values from 1 to 2.5
- impedance: bfloat16 [128, 256, 1024], P(('grp', 'gx'), None, 'gy'), may hold values from 0.5 to 2
Outputs:
- pressure: float32 [128, 256, 1024], P(('grp', 'gx'), None, 'gy')
- velocity: float32 [3, 128, 256, 1024], P(None, ('grp', 'gx'), None, 'gy')
All inputs are finite; a program needn't handle non-finite values.
Results may differ from a plain program's by a relative error of at most 0.0017.
Values may be sent and summed in bfloat16 or wider, within the bound.
A program may use at most 128 MiB of HBM per device.

v0:
```python
import jax
import jax.numpy as jnp
from jax import lax
from jax.sharding import PartitionSpec as P

courant = 0.15


def shortened(x):
    return jax.tree.map(lambda a: a.astype(jnp.bfloat16) if a.dtype == jnp.float32 else a, x)


def passed_along(block, axis, distance):
    devices = range(lax.axis_size(axis))
    route = [(i - distance, i) for i in devices if i - distance in devices]
    return lax.ppermute(block, axis, route)


def forward_diff(field, dim):
    widths = [(0, 0)] * field.ndim
    widths[dim] = (0, 1)
    padded = jnp.pad(field, widths)
    return lax.slice_in_dim(padded, 1, field.shape[dim] + 1, axis=dim) - field


def backward_diff(field, dim):
    widths = [(0, 0)] * field.ndim
    widths[dim] = (1, 0)
    padded = jnp.pad(field, widths)
    return field - lax.slice_in_dim(padded, 0, field.shape[dim], axis=dim)


def on_device(source, speed, impedance):
    count, whole_x, brick_y, depth = source.shape
    acoustic = lax.all_to_all(source, ("grp", "gx"), split_axis=1, concat_axis=2, tiled=True)
    sound = speed.astype(jnp.float32)
    imped = impedance.astype(jnp.float32)
    stiff = sound * imped
    buoy = sound / imped
    pressure = jnp.zeros(speed.shape, jnp.float32)
    vel_x = jnp.zeros(speed.shape, jnp.float32)
    vel_y = jnp.zeros(speed.shape, jnp.float32)
    vel_z = jnp.zeros(speed.shape, jnp.float32)
    for step in range(count):
        pressure = pressure + acoustic[count - 1 - step].astype(jnp.float32)
        loaded = stiff * pressure
        above_x = passed_along(shortened(loaded[0:1]), ("grp", "gx"), -1)
        above_z = passed_along(loaded[:, :, 0:1], "gy", -1)
        vel_x = vel_x + courant * (jnp.concatenate([loaded[1:], above_x], 0) - loaded)
        vel_y = vel_y + courant * forward_diff(loaded, 1)
        vel_z = vel_z + courant * (jnp.concatenate([loaded[:, :, 1:], above_z], 2) - loaded)
        flux_x = buoy * vel_x
        flux_y = buoy * vel_y
        flux_z = buoy * vel_z
        below_x = passed_along(shortened(flux_x[-1:]), ("grp", "gx"), 1)
        below_z = passed_along(flux_z[:, :, -1:], "gy", 1)
        spread = flux_x - jnp.concatenate([below_x, flux_x[:-1]], 0)
        spread = spread + backward_diff(flux_y, 1)
        spread = spread + flux_z - jnp.concatenate([below_z, flux_z[:, :, :-1]], 2)
        pressure = pressure + courant * spread
    return (pressure, jnp.stack([vel_x, vel_y, vel_z]))


def solution(mesh):
    in_specs = (
        P(None, None, ("grp", "gx"), "gy"),
        P(("grp", "gx"), None, "gy"),
        P(("grp", "gx"), None, "gy"),
    )
    out_specs = (P(("grp", "gx"), None, "gy"), P(None, ("grp", "gx"), None, "gy"))
    return jax.shard_map(
        on_device, mesh=mesh, in_specs=in_specs, out_specs=out_specs, check_vma=False
    )
```

profile of v0, /device:TPU:33, one launch (start us, length us, event | category | flops | bytes accessed | tf_op | source)
XLA Modules:
  0.0 196.3 jit_solution(5756416123559566129)
XLA Ops:
  0.6 1.4 copy.6
  2.0 41.2 %all_to_all.15 = bf16[4,128,8,128]{3,2,0,1:T(8,128)(2,1)S(1)} all-to-all(bf16[4,128,8,128]{3,2,0,1:T(8,128)(2,1)S(1)} %copy.6), channel_id=1, replica_groups=mesh['grp'=2,'gx'=16,'gy'=8] {'grp','gx'}, dimensions={1} | all-to-all | bytes 2097152 | tf_op jit(solution)/shard_map/all_to_all | solution.py:35
  43.2 0.3 slice_convert_fusion.3
  43.5 0.7 copy-done
  44.3 1.9 collective-permute-start
  46.3 2.3 %collective-permute-start.2 = (f32[4,256,1]{2,1,0:T(8,128)S(1)}, f32[4,256,1]{2,1,0:T(8,128)S(1)}, u32[]{:S(2)}, u32[]{:S(2)}) collective-permute-start(f32[4,256,1]{2,1,0:T(8,128)S(1)} %bitcast.29), channel_id=1, source_target_pairs={{1,0},{2,1},{3,2},{4,3},{5,4},{6,5},{7,6},{9,8},{10,9},{11,10},{12... | collective-permute-start | bytes 12296 | tf_op jit(solution)/shard_map/ppermute | solution.py:16
  48.6 0.2 slice.193
  48.8 0.5 collective-permute-done
  49.3 13.0 %collective-permute-done.2 = f32[4,256,1]{2,1,0:T(8,128)S(1)} collective-permute-done((f32[4,256,1]{2,1,0:T(8,128)S(1)}, f32[4,256,1]{2,1,0:T(8,128)S(1)}, u32[]{:S(2)}, u32[]{:S(2)}) %collective-permute-start.2) | collective-permute-done | bytes 4128 | tf_op jit(solution)/shard_map/ppermute | solution.py:16
  62.3 0.3 fusion.56
  62.7 2.3 %collective-permute-start.1 = (bf16[1,256,128]{2,1,0:T(8,128)(2,1)S(1)}, bf16[1,256,128]{2,1,0:T(8,128)(2,1)S(1)}, u32[]{:S(2)}, u32[]{:S(2)}) collective-permute-start(bf16[1,256,128]{2,1,0:T(8,128)(2,1)S(1)} %slice.334), channel_id=1, source_target_pairs={{0,8},{8,16},{16,24},{24,32},{32,40},{40,48},{48,56},{56,64},{64,7... | collective-permute-start | bytes 196616 | tf_op jit(solution)/shard_map/ppermute | solution.py:16
  65.0 0.2 slice.195
  65.2 2.2 %collective-permute-start.3 = (f32[4,256,1]{2,1,0:T(8,128)S(1)}, f32[4,256,1]{2,1,0:T(8,128)S(1)}, u32[]{:S(2)}, u32[]{:S(2)}) collective-permute-start(f32[4,256,1]{2,1,0:T(8,128)S(1)} %slice.195), channel_id=1, source_target_pairs={{0,1},{1,2},{2,3},{3,4},{4,5},{5,6},{6,7},{8,9},{9,10},{10,11},{11... | collective-permute-start | bytes 12296 | tf_op jit(solution)/shard_map/ppermute | solution.py:16
  67.5 5.4 %collective-permute-done.1 = bf16[1,256,128]{2,1,0:T(8,128)(2,1)S(1)} collective-permute-done((bf16[1,256,128]{2,1,0:T(8,128)(2,1)S(1)}, bf16[1,256,128]{2,1,0:T(8,128)(2,1)S(1)}, u32[]{:S(2)}, u32[]{:S(2)}) %collective-permute-start.1) | collective-permute-done | bytes 65568 | tf_op jit(solution)/shard_map/ppermute | solution.py:16
  72.9 5.3 %collective-permute-done.3 = f32[4,256,1]{2,1,0:T(8,128)S(1)} collective-permute-done((f32[4,256,1]{2,1,0:T(8,128)S(1)}, f32[4,256,1]{2,1,0:T(8,128)S(1)}, u32[]{:S(2)}, u32[]{:S(2)}) %collective-permute-start.3) | collective-permute-done | bytes 4128 | tf_op jit(solution)/shard_map/ppermute | solution.py:16
  78.2 0.4 fusion.54
  78.6 5.8 %collective-permute-start.4 = (bf16[1,256,128]{2,1,0:T(8,128)(2,1)S(1)}, bf16[1,256,128]{2,1,0:T(8,128)(2,1)S(1)}, u32[]{:S(2)}, u32[]{:S(2)}) collective-permute-start(bf16[1,256,128]{2,1,0:T(8,128)(2,1)S(1)} %slice.333), channel_id=1, source_target_pairs={{8,0},{16,8},{24,16},{32,24},{40,32},{48,40},{56,48},{64,56},{72,6... | collective-permute-start | bytes 196616 | tf_op jit(solution)/shard_map/ppermute | solution.py:16
  84.4 1.9 collective-permute-start.6
  86.4 0.2 slice.202
  86.6 13.5 %collective-permute-done.6 = f32[4,256,1]{2,1,0:T(8,128)S(1)} collective-permute-done((f32[4,256,1]{2,1,0:T(8,128)S(1)}, f32[4,256,1]{2,1,0:T(8,128)S(1)}, u32[]{:S(2)}, u32[]{:S(2)}) %collective-permute-start.6) | collective-permute-done | bytes 4128 | tf_op jit(solution)/shard_map/ppermute | solution.py:16
  100.1 0.6 fusion.68
  100.8 1.9 collective-permute-start.5
  102.7 0.2 slice.204
  102.9 3.6 %collective-permute-start.7 = (f32[4,256,1]{2,1,0:T(8,128)S(1)}, f32[4,256,1]{2,1,0:T(8,128)S(1)}, u32[]{:S(2)}, u32[]{:S(2)}) collective-permute-start(f32[4,256,1]{2,1,0:T(8,128)S(1)} %slice.204), channel_id=1, source_target_pairs={{0,1},{1,2},{2,3},{3,4},{4,5},{5,6},{6,7},{8,9},{9,10},{10,11},{11... | collective-permute-start | bytes 12296 | tf_op jit(solution)/shard_map/ppermute | solution.py:16
  106.5 4.5 %collective-permute-done.5 = bf16[1,256,128]{2,1,0:T(8,128)(2,1)S(1)} collective-permute-done((bf16[1,256,128]{2,1,0:T(8,128)(2,1)S(1)}, bf16[1,256,128]{2,1,0:T(8,128)(2,1)S(1)}, u32[]{:S(2)}, u32[]{:S(2)}) %collective-permute-start.5) | collective-permute-done | bytes 65568 | tf_op jit(solution)/shard_map/ppermute | solution.py:16
  111.0 7.3 %collective-permute-done.7 = f32[4,256,1]{2,1,0:T(8,128)S(1)} collective-permute-done((f32[4,256,1]{2,1,0:T(8,128)S(1)}, f32[4,256,1]{2,1,0:T(8,128)S(1)}, u32[]{:S(2)}, u32[]{:S(2)}) %collective-permute-start.7) | collective-permute-done | bytes 4128 | tf_op jit(solution)/shard_map/ppermute | solution.py:16
  118.4 0.4 fusion.53
  118.7 7.3 %collective-permute-start.8 = (bf16[1,256,128]{2,1,0:T(8,128)(2,1)S(1)}, bf16[1,256,128]{2,1,0:T(8,128)(2,1)S(1)}, u32[]{:S(2)}, u32[]{:S(2)}) collective-permute-start(bf16[1,256,128]{2,1,0:T(8,128)(2,1)S(1)} %slice.331), channel_id=1, source_target_pairs={{8,0},{16,8},{24,16},{32,24},{40,32},{48,40},{56,48},{64,56},{72,6... | collective-permute-start | bytes 196616 | tf_op jit(solution)/shard_map/ppermute | solution.py:16
  126.0 1.9 collective-permute-start.10
  128.2 0.5 collective-permute-done.8
  128.7 8.9 %collective-permute-done.10 = f32[4,256,1]{2,1,0:T(8,128)S(1)} collective-permute-done((f32[4,256,1]{2,1,0:T(8,128)S(1)}, f32[4,256,1]{2,1,0:T(8,128)S(1)}, u32[]{:S(2)}, u32[]{:S(2)}) %collective-permute-start.10) | collective-permute-done | bytes 4128 | tf_op jit(solution)/shard_map/ppermute | solution.py:16
  137.6 0.4 fusion.65
  138.1 2.0 %collective-permute-start.9 = (bf16[1,256,128]{2,1,0:T(8,128)(2,1)S(1)}, bf16[1,256,128]{2,1,0:T(8,128)(2,1)S(1)}, u32[]{:S(2)}, u32[]{:S(2)}) collective-permute-start(bf16[1,256,128]{2,1,0:T(8,128)(2,1)S(1)} %slice.330), channel_id=1, source_target_pairs={{0,8},{8,16},{16,24},{24,32},{32,40},{40,48},{48,56},{56,64},{64,7... | collective-permute-start | bytes 196616 | tf_op jit(solution)/shard_map/ppermute | solution.py:16
  140.3 5.0 %collective-permute-start.11 = (f32[4,256,1]{2,1,0:T(8,128)S(1)}, f32[4,256,1]{2,1,0:T(8,128)S(1)}, u32[]{:S(2)}, u32[]{:S(2)}) collective-permute-start(f32[4,256,1]{2,1,0:T(8,128)S(1)} %slice.213), channel_id=1, source_target_pairs={{0,1},{1,2},{2,3},{3,4},{4,5},{5,6},{6,7},{8,9},{9,10},{10,11},{11... | collective-permute-start | bytes 12296 | tf_op jit(solution)/shard_map/ppermute | solution.py:16
  145.3 3.4 %collective-permute-done.9 = bf16[1,256,128]{2,1,0:T(8,128)(2,1)S(1)} collective-permute-done((bf16[1,256,128]{2,1,0:T(8,128)(2,1)S(1)}, bf16[1,256,128]{2,1,0:T(8,128)(2,1)S(1)}, u32[]{:S(2)}, u32[]{:S(2)}) %collective-permute-start.9) | collective-permute-done | bytes 65568 | tf_op jit(solution)/shard_map/ppermute | solution.py:16
  148.7 7.7 %collective-permute-done.11 = f32[4,256,1]{2,1,0:T(8,128)S(1)} collective-permute-done((f32[4,256,1]{2,1,0:T(8,128)S(1)}, f32[4,256,1]{2,1,0:T(8,128)S(1)}, u32[]{:S(2)}, u32[]{:S(2)}) %collective-permute-start.11) | collective-permute-done | bytes 4128 | tf_op jit(solution)/shard_map/ppermute | solution.py:16
  156.4 0.4 fusion.52
  156.9 4.6 %collective-permute-start.12 = (bf16[1,256,128]{2,1,0:T(8,128)(2,1)S(1)}, bf16[1,256,128]{2,1,0:T(8,128)(2,1)S(1)}, u32[]{:S(2)}, u32[]{:S(2)}) collective-permute-start(bf16[1,256,128]{2,1,0:T(8,128)(2,1)S(1)} %slice.329), channel_id=1, source_target_pairs={{8,0},{16,8},{24,16},{32,24},{40,32},{48,40},{56,48},{64,56},{72,6... | collective-permute-start | bytes 196616 | tf_op jit(solution)/shard_map/ppermute | solution.py:16
  161.5 1.9 collective-permute-start.14
  163.7 12.8 %collective-permute-done.14 = f32[4,256,1]{2,1,0:T(8,128)S(1)} collective-permute-done((f32[4,256,1]{2,1,0:T(8,128)S(1)}, f32[4,256,1]{2,1,0:T(8,128)S(1)}, u32[]{:S(2)}, u32[]{:S(2)}) %collective-permute-start.14) | collective-permute-done | bytes 4128 | tf_op jit(solution)/shard_map/ppermute | solution.py:16
  176.5 0.5 fusion.60
  176.9 1.9 collective-permute-start.13
  178.9 0.2 slice.222
  179.1 5.0 %collective-permute-start.15 = (f32[4,256,1]{2,1,0:T(8,128)S(1)}, f32[4,256,1]{2,1,0:T(8,128)S(1)}, u32[]{:S(2)}, u32[]{:S(2)}) collective-permute-start(f32[4,256,1]{2,1,0:T(8,128)S(1)} %slice.222), channel_id=1, source_target_pairs={{0,1},{1,2},{2,3},{3,4},{4,5},{5,6},{6,7},{8,9},{9,10},{10,11},{11... | collective-permute-start | bytes 12296 | tf_op jit(solution)/shard_map/ppermute | solution.py:16
  184.1 1.3 pad_maximum_fusion
  185.4 1.6 collective-permute-done.13
  187.1 8.1 %collective-permute-done.15 = f32[4,256,1]{2,1,0:T(8,128)S(1)} collective-permute-done((f32[4,256,1]{2,1,0:T(8,128)S(1)}, f32[4,256,1]{2,1,0:T(8,128)S(1)}, u32[]{:S(2)}, u32[]{:S(2)}) %collective-permute-start.15) | collective-permute-done | bytes 4128 | tf_op jit(solution)/shard_map/ppermute | solution.py:16
  195.2 1.1 fusion.37
  (33 shorter events, 1.1 us)
Async XLA Ops:
  43.2 1.0 copy-start
  43.2 1.0 copy-start.1
  44.3 5.0 %collective-permute-start = (bf16[1,256,128]{2,1,0:T(8,128)(2,1)S(1)}, bf16[1,256,128]{2,1,0:T(8,128)(2,1)S(1)}, u32[]{:S(2)}, u32[]{:S(2)}) collective-permute-start(bf16[1,256,128]{2,1,0:T(8,128)(2,1)S(1)} %slice.335), channel_id=1, source_target_pairs={{8,0},{16,8},{24,16},{32,24},{40,32},{48,40},{56,48},{64,56},{72,6... | collective-permute-start | bytes 196616 | tf_op jit(solution)/shard_map/ppermute | solution.py:16
  46.3 16.1 %collective-permute-start.2 = (f32[4,256,1]{2,1,0:T(8,128)S(1)}, f32[4,256,1]{2,1,0:T(8,128)S(1)}, u32[]{:S(2)}, u32[]{:S(2)}) collective-permute-start(f32[4,256,1]{2,1,0:T(8,128)S(1)} %bitcast.29), channel_id=1, source_target_pairs={{1,0},{2,1},{3,2},{4,3},{5,4},{6,5},{7,6},{9,8},{10,9},{11,10},{12... | collective-permute-start | bytes 12296 | tf_op jit(solution)/shard_map/ppermute | solution.py:16
  62.7 10.2 %collective-permute-start.1 = (bf16[1,256,128]{2,1,0:T(8,128)(2,1)S(1)}, bf16[1,256,128]{2,1,0:T(8,128)(2,1)S(1)}, u32[]{:S(2)}, u32[]{:S(2)}) collective-permute-start(bf16[1,256,128]{2,1,0:T(8,128)(2,1)S(1)} %slice.334), channel_id=1, source_target_pairs={{0,8},{8,16},{16,24},{24,32},{32,40},{40,48},{48,56},{56,64},{64,7... | collective-permute-start | bytes 196616 | tf_op jit(solution)/shard_map/ppermute | solution.py:16
  65.2 13.0 %collective-permute-start.3 = (f32[4,256,1]{2,1,0:T(8,128)S(1)}, f32[4,256,1]{2,1,0:T(8,128)S(1)}, u32[]{:S(2)}, u32[]{:S(2)}) collective-permute-start(f32[4,256,1]{2,1,0:T(8,128)S(1)} %slice.195), channel_id=1, source_target_pairs={{0,1},{1,2},{2,3},{3,4},{4,5},{5,6},{6,7},{8,9},{9,10},{10,11},{11... | collective-permute-start | bytes 12296 | tf_op jit(solution)/shard_map/ppermute | solution.py:16
  78.6 7.9 %collective-permute-start.4 = (bf16[1,256,128]{2,1,0:T(8,128)(2,1)S(1)}, bf16[1,256,128]{2,1,0:T(8,128)(2,1)S(1)}, u32[]{:S(2)}, u32[]{:S(2)}) collective-permute-start(bf16[1,256,128]{2,1,0:T(8,128)(2,1)S(1)} %slice.333), channel_id=1, source_target_pairs={{8,0},{16,8},{24,16},{32,24},{40,32},{48,40},{56,48},{64,56},{72,6... | collective-permute-start | bytes 196616 | tf_op jit(solution)/shard_map/ppermute | solution.py:16
  84.4 15.7 %collective-permute-start.6 = (f32[4,256,1]{2,1,0:T(8,128)S(1)}, f32[4,256,1]{2,1,0:T(8,128)S(1)}, u32[]{:S(2)}, u32[]{:S(2)}) collective-permute-start(f32[4,256,1]{2,1,0:T(8,128)S(1)} %bitcast.36), channel_id=1, source_target_pairs={{1,0},{2,1},{3,2},{4,3},{5,4},{6,5},{7,6},{9,8},{10,9},{11,10},{12... | collective-permute-start | bytes 12296 | tf_op jit(solution)/shard_map/ppermute | solution.py:16
  100.8 10.3 %collective-permute-start.5 = (bf16[1,256,128]{2,1,0:T(8,128)(2,1)S(1)}, bf16[1,256,128]{2,1,0:T(8,128)(2,1)S(1)}, u32[]{:S(2)}, u32[]{:S(2)}) collective-permute-start(bf16[1,256,128]{2,1,0:T(8,128)(2,1)S(1)} %slice.332), channel_id=1, source_target_pairs={{0,8},{8,16},{16,24},{24,32},{32,40},{40,48},{48,56},{56,64},{64,7... | collective-permute-start | bytes 196616 | tf_op jit(solution)/shard_map/ppermute | solution.py:16
  102.9 15.5 %collective-permute-start.7 = (f32[4,256,1]{2,1,0:T(8,128)S(1)}, f32[4,256,1]{2,1,0:T(8,128)S(1)}, u32[]{:S(2)}, u32[]{:S(2)}) collective-permute-start(f32[4,256,1]{2,1,0:T(8,128)S(1)} %slice.204), channel_id=1, source_target_pairs={{0,1},{1,2},{2,3},{3,4},{4,5},{5,6},{6,7},{8,9},{9,10},{10,11},{11... | collective-permute-start | bytes 12296 | tf_op jit(solution)/shard_map/ppermute | solution.py:16
  118.7 10.0 %collective-permute-start.8 = (bf16[1,256,128]{2,1,0:T(8,128)(2,1)S(1)}, bf16[1,256,128]{2,1,0:T(8,128)(2,1)S(1)}, u32[]{:S(2)}, u32[]{:S(2)}) collective-permute-start(bf16[1,256,128]{2,1,0:T(8,128)(2,1)S(1)} %slice.331), channel_id=1, source_target_pairs={{8,0},{16,8},{24,16},{32,24},{40,32},{48,40},{56,48},{64,56},{72,6... | collective-permute-start | bytes 196616 | tf_op jit(solution)/shard_map/ppermute | solution.py:16
  126.0 11.6 %collective-permute-start.10 = (f32[4,256,1]{2,1,0:T(8,128)S(1)}, f32[4,256,1]{2,1,0:T(8,128)S(1)}, u32[]{:S(2)}, u32[]{:S(2)}) collective-permute-start(f32[4,256,1]{2,1,0:T(8,128)S(1)} %bitcast.34), channel_id=1, source_target_pairs={{1,0},{2,1},{3,2},{4,3},{5,4},{6,5},{7,6},{9,8},{10,9},{11,10},{12... | collective-permute-start | bytes 12296 | tf_op jit(solution)/shard_map/ppermute | solution.py:16
  138.1 10.6 %collective-permute-start.9 = (bf16[1,256,128]{2,1,0:T(8,128)(2,1)S(1)}, bf16[1,256,128]{2,1,0:T(8,128)(2,1)S(1)}, u32[]{:S(2)}, u32[]{:S(2)}) collective-permute-start(bf16[1,256,128]{2,1,0:T(8,128)(2,1)S(1)} %slice.330), channel_id=1, source_target_pairs={{0,8},{8,16},{16,24},{24,32},{32,40},{40,48},{48,56},{56,64},{64,7... | collective-permute-start | bytes 196616 | tf_op jit(solution)/shard_map/ppermute | solution.py:16
  140.3 16.1 %collective-permute-start.11 = (f32[4,256,1]{2,1,0:T(8,128)S(1)}, f32[4,256,1]{2,1,0:T(8,128)S(1)}, u32[]{:S(2)}, u32[]{:S(2)}) collective-permute-start(f32[4,256,1]{2,1,0:T(8,128)S(1)} %slice.213), channel_id=1, source_target_pairs={{0,1},{1,2},{2,3},{3,4},{4,5},{5,6},{6,7},{8,9},{9,10},{10,11},{11... | collective-permute-start | bytes 12296 | tf_op jit(solution)/shard_map/ppermute | solution.py:16
  156.9 6.8 %collective-permute-start.12 = (bf16[1,256,128]{2,1,0:T(8,128)(2,1)S(1)}, bf16[1,256,128]{2,1,0:T(8,128)(2,1)S(1)}, u32[]{:S(2)}, u32[]{:S(2)}) collective-permute-start(bf16[1,256,128]{2,1,0:T(8,128)(2,1)S(1)} %slice.329), channel_id=1, source_target_pairs={{8,0},{16,8},{24,16},{32,24},{40,32},{48,40},{56,48},{64,56},{72,6... | collective-permute-start | bytes 196616 | tf_op jit(solution)/shard_map/ppermute | solution.py:16
  161.5 15.0 %collective-permute-start.14 = (f32[4,256,1]{2,1,0:T(8,128)S(1)}, f32[4,256,1]{2,1,0:T(8,128)S(1)}, u32[]{:S(2)}, u32[]{:S(2)}) collective-permute-start(f32[4,256,1]{2,1,0:T(8,128)S(1)} %bitcast.35), channel_id=1, source_target_pairs={{1,0},{2,1},{3,2},{4,3},{5,4},{6,5},{7,6},{9,8},{10,9},{11,10},{12... | collective-permute-start | bytes 12296 | tf_op jit(solution)/shard_map/ppermute | solution.py:16
  176.9 10.1 %collective-permute-start.13 = (bf16[1,256,128]{2,1,0:T(8,128)(2,1)S(1)}, bf16[1,256,128]{2,1,0:T(8,128)(2,1)S(1)}, u32[]{:S(2)}, u32[]{:S(2)}) collective-permute-start(bf16[1,256,128]{2,1,0:T(8,128)(2,1)S(1)} %slice.328), channel_id=1, source_target_pairs={{0,8},{8,16},{16,24},{24,32},{32,40},{40,48},{48,56},{56,64},{64,7... | collective-permute-start | bytes 196616 | tf_op jit(solution)/shard_map/ppermute | solution.py:16
  179.1 16.1 %collective-permute-start.15 = (f32[4,256,1]{2,1,0:T(8,128)S(1)}, f32[4,256,1]{2,1,0:T(8,128)S(1)}, u32[]{:S(2)}, u32[]{:S(2)}) collective-permute-start(f32[4,256,1]{2,1,0:T(8,128)S(1)} %slice.222), channel_id=1, source_target_pairs={{0,1},{1,2},{2,3},{3,4},{4,5},{5,6},{6,7},{8,9},{9,10},{10,11},{11... | collective-permute-start | bytes 12296 | tf_op jit(solution)/shard_map/ppermute | solution.py:16
where the time goes:
time: 200 us; the launch traced here: 196 us
  waiting for transfers between devices  92.5 us (46%)
  starting transfers between devices  51.8 us (26%)
  blocking collectives  41.2 us (21%)
  other arithmetic  5.78 us (3%)
  local copies, waits for them, and re-layouts  4.06 us (2%)
    ppermute x16, waiting for transfers between devices, passed_along(): return lax.ppermute(block, axis, route)  92.5 us
    ppermute x16, starting transfers between devices, passed_along(): return lax.ppermute(block, axis, route)  51.8 us
    all_to_all x1, blocking collectives, on_device(): lax.all_to_all(source, ('grp', 'gx'), split_axis=1, concat_axis=2, tiled=...  41.2 us
  transfers between devices with their start and end apart: 16, of which 14 were waited for; matrix products, arithmetic and copies ran while one was open for 2% of the time, Pallas kernels for 0%

commit v1 on v0

v1 whole, which is shorter than its diff:
```python
import jax
import jax.numpy as jnp
from jax import lax
from jax.experimental import pallas as pl
from jax.experimental.pallas import tpu as pltpu
from jax.sharding import PartitionSpec as P

courant = 0.15
MESH = pl.DeviceIdType.MESH
SLABS = 32
F32 = jnp.float32
BF16 = jnp.bfloat16


def slab_device(slab, gy):
    return (slab // 16, lax.rem(slab, 16), gy)


def rounded(x):
    return x.astype(BF16).astype(F32)


def packed(layer_of):
    row = lax.broadcasted_iota(jnp.int32, (16, 128), 0)
    lane = lax.broadcasted_iota(jnp.int32, (16, 128), 1)

    def add(j, total):
        pick = ((row == j) & (lane == 0)) | ((row == 8 + j) & (lane == 127))
        return total + lax.dot_general(
            jnp.where(pick, 1.0, 0.0).astype(BF16),
            layer_of(j),
            (((1,), (1,)), ((), ())),
            preferred_element_type=F32,
        )

    return lax.fori_loop(0, 8, add, jnp.zeros((16, 128), F32))


def kernel(src, speed, imp, pres, vel, acc, hs, sx, hx, zc, hc, zs, hz, stiff, buoy, p, vx, fx, load, fy, edge, vzm,
           send, recv, own_sem, cs_send, cs_recv, cz_send, cz_recv, x_send, x_recv, z_send, z_recv):
    gy = lax.axis_index("gy")
    s = lax.axis_index("grp") * 16 + lax.axis_index("gx")
    above, below = lax.rem(s + 1, SLABS), lax.rem(s + SLABS - 1, SLABS)
    z_above, z_below = lax.rem(gy + 1, 8), lax.rem(gy + 7, 8)
    x_to = (slab_device(above, gy), slab_device(below, gy))
    z_to = (slab_device(s, z_above), slab_device(s, z_below))

    barrier = pltpu.get_barrier_semaphore()

    def greet(d, _):
        pl.semaphore_signal(barrier, inc=1, device_id=slab_device(lax.rem(s + d, SLABS), gy), device_id_type=MESH)
        return 0

    lax.fori_loop(1, SLABS, greet, 0)
    for to in z_to:
        pl.semaphore_signal(barrier, inc=1, device_id=to, device_id_type=MESH)

    own = pltpu.make_async_copy(src.at[:, pl.ds(32 * s, 32)], acc.at[:, pl.ds(32 * s, 32)], own_sem)
    own.start()

    def coefficients(l, _):
        a, b = speed[l].astype(F32), imp[l].astype(F32)
        stiff[l + 1] = a * b
        buoy[l + 1] = a / b
        vel[0, l] = jnp.zeros((256, 128), F32)
        vel[1, l] = jnp.zeros((256, 128), F32)
        vel[2, l] = jnp.zeros((256, 128), F32)
        load[l + 1, 256:264] = jnp.zeros((8, 128), F32)
        return 0

    lax.fori_loop(0, 4, coefficients, 0)

    def zero_vx(l, _):
        vx[l] = jnp.zeros((256, 128), F32)
        return 0

    lax.fori_loop(0, 5, zero_vx, 0)
    fy[0:8] = jnp.zeros((8, 128), F32)
    vzm[...] = jnp.zeros((8, 128), F32)

    def half(ref, j):
        return ref[j // 2, pl.ds(pl.multiple_of(128 * lax.rem(j, 2), 128), 128)]

    packed_speed = packed(lambda j: half(speed, j))
    packed_imp = packed(lambda j: half(imp, j))
    zc[0, 0:8] = packed_speed[8:16]
    zc[0, 8:16] = packed_imp[8:16]
    zc[1, 0:8] = packed_speed[0:8]
    zc[1, 8:16] = packed_imp[0:8]

    pl.semaphore_wait(barrier, SLABS - 1 + 2)

    def exchange(n):
        def one(d, _):
            to = lax.rem(s + d, SLABS)
            pltpu.make_async_remote_copy(
                src.at[3 - n, pl.ds(32 * to, 32)], acc.at[3 - n, pl.ds(32 * s, 32)], send, recv.at[n],
                device_id=slab_device(to, gy), device_id_type=MESH).start()
            return 0

        lax.fori_loop(1, SLABS, one, 0)

    exchange(0)
    halo = []
    for way in range(2):
        layer = 3 - 3 * way
        for k, field in enumerate((speed, imp)):
            halo.append(pltpu.make_async_remote_copy(
                field.at[layer], hs.at[2 * way + k], cs_send.at[2 * way + k], cs_recv.at[2 * way + k],
                device_id=x_to[way], device_id_type=MESH))
        halo.append(pltpu.make_async_remote_copy(
            zc.at[way], hc.at[way], cz_send.at[way], cz_recv.at[way], device_id=z_to[way], device_id_type=MESH))
    for copy in halo:
        copy.start()
    for n in range(1, 4):
        exchange(n)
    own.wait()
    sent = []
    lane = lax.broadcasted_iota(jnp.int32, (256, 128), 1)
    has_below, has_above = jnp.where(s > 0, 1.0, 0.0), jnp.where(s < SLABS - 1, 1.0, 0.0)
    has_z_below, has_z_above = jnp.where(gy > 0, 1.0, 0.0), jnp.where(gy < 7, 1.0, 0.0)

    for n in range(4):
        pltpu.make_async_copy(acc.at[3 - n, 0:32 * 31], acc.at[3 - n, 0:32 * 31], recv.at[n]).wait()

        def add_source(b, _):
            x = acc[3 - n, pl.ds(pl.multiple_of(32 * b, 32), 32)].astype(F32).reshape(4, 8, 128)
            rows = pl.ds(pl.multiple_of(8 * b, 8), 8)
            p[1:5, rows] = x if n == 0 else p[1:5, rows] + x
            return 0

        lax.fori_loop(0, SLABS, add_source, 0)
        sx[n, 0] = p[4].astype(BF16)
        sx[n, 1] = p[1].astype(BF16)
        columns = packed(lambda j: half(p.at[1:5], j).astype(BF16))
        zs[n, 0] = columns[8:16]
        zs[n, 1] = columns[0:8]
        copies = []
        for way in range(2):
            copies.append(pltpu.make_async_remote_copy(
                sx.at[n, way], hx.at[n, way], x_send.at[n, way], x_recv.at[n, way],
                device_id=x_to[way], device_id_type=MESH))
            copies.append(pltpu.make_async_remote_copy(
                zs.at[n, way], hz.at[n, way], z_send.at[n, way], z_recv.at[n, way],
                device_id=z_to[way], device_id_type=MESH))
        for copy in copies:
            copy.start()
        if n == 0:
            for copy in halo:
                copy.wait_recv()
            stiff[0] = hs[0].astype(F32) * hs[1].astype(F32)
            buoy[0] = hs[0].astype(F32) / hs[1].astype(F32) * has_below
            stiff[5] = hs[2].astype(F32) * hs[3].astype(F32) * has_above
        for copy in copies:
            copy.wait_recv()
        sent += copies
        p[0] = hx[n, 0].astype(F32)
        p[5] = hx[n, 1].astype(F32)

        past = hc[1, 0:8] * hc[1, 8:16] * hz[n, 1] * has_z_above
        vzm[...] += courant * (zc[1, 0:8] * zc[1, 8:16] * zs[n, 1] - hc[0, 0:8] * hc[0, 8:16] * hz[n, 0])
        before = hc[0, 0:8] / hc[0, 8:16] * vzm[...] * has_z_below
        rows = jnp.concatenate(
            [rounded(past), past - rounded(past), rounded(before), before - rounded(before)], 0)
        columns = jnp.transpose(rows).astype(BF16)
        row32 = lax.broadcasted_iota(jnp.int32, (32, 128), 0)
        lane32 = lax.broadcasted_iota(jnp.int32, (32, 128), 1)

        def spread_edge(j, _):
            pick = (((row32 == j) | (row32 == 8 + j)) & (lane32 == 127)) | (
                ((row32 == 16 + j) | (row32 == 24 + j)) & (lane32 == 0))
            edge[j // 2, pl.ds(pl.multiple_of(128 * lax.rem(j, 2), 128), 128)] = jnp.dot(
                columns, jnp.where(pick, 1.0, 0.0).astype(BF16), preferred_element_type=F32)
            return 0

        lax.fori_loop(0, 8, spread_edge, 0)

        def loads(l, _):
            load[l, 0:256] = stiff[l] * p[l]
            return 0

        lax.fori_loop(0, 6, loads, 0)

        def x_part(l, _):
            v = vx[l] + courant * (load[l + 1, 0:256] - load[l, 0:256])
            vx[l] = v
            fx[l] = buoy[l] * v
            return 0

        lax.fori_loop(0, 5, x_part, 0)

        def layer(l, _):
            b = buoy[l + 1]
            here = load[l + 1, 0:256]
            v1 = vel[1, l] + courant * (load[l + 1, 1:257] - here)
            vel[1, l] = v1
            flux = b * v1
            fy[8:264] = flux
            total = (fx[l + 1] - fx[l]) + (flux - fy[7:263])
            rim = edge[l]
            v2 = vel[2, l] + courant * (jnp.where(lane == 127, rim, pltpu.roll(here, 127, 1)) - here)
            vel[2, l] = v2
            flux = b * v2
            total = total + (flux - jnp.where(lane == 0, rim, pltpu.roll(flux, 1, 1)))
            out = p[l + 1] + courant * total
            if n < 3:
                p[l + 1] = out
            else:
                pres[l] = out
                vel[0, l] = vx[l + 1]
            return 0

        lax.fori_loop(0, 4, layer, 0)

    for copy in halo + sent:
        copy.wait_send()
    pltpu.make_async_copy(acc.at[:, 0:32 * 31], acc.at[:, 0:32 * 31], send).wait()


def on_device(source, speed, impedance):
    vmem = pl.BlockSpec(memory_space=pltpu.VMEM)
    dma = pltpu.SemaphoreType.DMA
    return pl.pallas_call(
        kernel,
        out_shape=(
            jax.ShapeDtypeStruct((4, 256, 128), F32),
            jax.ShapeDtypeStruct((3, 4, 256, 128), F32),
        ),
        in_specs=[pl.BlockSpec(memory_space=pl.ANY), vmem, vmem],
        out_specs=(vmem, vmem),
        scratch_shapes=[
            pltpu.VMEM((4, 1024, 128), BF16),
            pltpu.VMEM((4, 256, 128), BF16),
            pltpu.VMEM((4, 2, 256, 128), BF16),
            pltpu.VMEM((4, 2, 256, 128), BF16),
            pltpu.VMEM((2, 16, 128), F32),
            pltpu.VMEM((2, 16, 128), F32),
            pltpu.VMEM((4, 2, 8, 128), F32),
            pltpu.VMEM((4, 2, 8, 128), F32),
            pltpu.VMEM((6, 256, 128), F32),
            pltpu.VMEM((5, 256, 128), F32),
            pltpu.VMEM((6, 256, 128), F32),
            pltpu.VMEM((5, 256, 128), F32),
            pltpu.VMEM((5, 256, 128), F32),
            pltpu.VMEM((6, 264, 128), F32),
            pltpu.VMEM((264, 128), F32),
            pltpu.VMEM((4, 256, 128), F32),
            pltpu.VMEM((8, 128), F32),
            dma, dma((4,)), dma, dma((4,)), dma((4,)), dma((2,)), dma((2,)),
            dma((4, 2)), dma((4, 2)), dma((4, 2)), dma((4, 2)),
        ],
        compiler_params=pltpu.CompilerParams(
            collective_id=0, has_side_effects=True, vmem_limit_bytes=48 * 1024 * 1024),
    )(source.reshape(4, 1024, 128), speed, impedance)


def solution(mesh):
    in_specs = (
        P(None, None, ("grp", "gx"), "gy"),
        P(("grp", "gx"), None, "gy"),
        P(("grp", "gx"), None, "gy"),
    )
    out_specs = (P(("grp", "gx"), None, "gy"), P(None, ("grp", "gx"), None, "gy"))
    return jax.shard_map(on_device, mesh=mesh, in_specs=in_specs, out_specs=out_specs, check_vma=False)
```

time: 200 us -> 80.3 us (0.40); the launches traced: 196 us -> 80.1 us
  waiting for transfers between devices: 92.5 us -> 0 us
  Pallas kernels: 0 us -> 74.4 us
  starting transfers between devices: 51.8 us -> 0 us
  blocking collectives: 41.2 us -> 0 us
  other arithmetic: 5.78 us -> 0 us
    ppermute x16 -> x0, waiting for transfers between devices: 92.5 us -> none  [passed_along(): return lax.ppermute(block, axis, route)]
    pallas_call x0 -> x1, Pallas kernels: none -> 74.4 us  [on_device(): pl.pallas_call(kernel, out_shape=(jax.ShapeDtypeStruct((4, 256, 128), F32...]
    ppermute x16 -> x0, starting transfers between devices: 51.8 us -> none  [passed_along(): return lax.ppermute(block, axis, route)]
    all_to_all x1 -> x0, blocking collectives: 41.2 us -> none  [on_device(): lax.all_to_all(source, ('grp', 'gx'), split_axis=1, concat_axis=2, tiled=...]
    unnamed x5 -> x8, local copies, waits for them, and re-layouts: 2.16 us -> 5.05 us
    mul x7 -> x0, other arithmetic: 2.65 us -> none  [the longest x3 1.4 us: on_device(): flux_x = buoy * vel_x]
  transfers between devices with their start and end apart: 16 -> 0, of which waited for: 14 -> 0; matrix products, arithmetic and copies ran while one was open for 2% -> 0% of each run, Pallas kernels for 0% -> 0%
where the time goes in v1:
time: 80.3 us; the launch traced here: 80.1 us
  Pallas kernels  74.4 us (93%)
  local copies, waits for them, and re-layouts  5.05 us (6%)
    pallas_call x1, Pallas kernels, on_device(): pl.pallas_call(kernel, out_shape=(jax.ShapeDtypeStruct((4, 256, 128), F32...  74.4 us
    unnamed x8, local copies, waits for them, and re-layouts  5.05 us

profile of v1, /device:TPU:33, one launch (start us, length us, event | category | flops | bytes accessed | tf_op | source)
XLA Modules:
  0.0 80.1 jit_solution(9923451497465288141)
XLA Ops:
  0.6 0.0 copy-start
  0.6 1.2 %copy-done = bf16[4,128,8,128]{3,2,1,0:T(8,128)(2,1)S(1)} copy-done((bf16[4,128,8,128]{3,2,1,0:T(8,128)(2,1)S(1)}, bf16[4,128,8,128]{3,2,1,0:T(8,128)(2,1)}, u32[]{:S(2)}) %copy-start) | copy-done | bytes 1048600
  1.9 0.0 copy-start.1
  1.9 0.9 %copy-done.1 = bf16[4,256,128]{2,1,0:T(8,128)(2,1)S(1)} copy-done((bf16[4,256,128]{2,1,0:T(8,128)(2,1)S(1)}, bf16[4,256,128]{2,1,0:T(8,128)(2,1)}, u32[]{:S(2)}) %copy-start.1) | copy-done | bytes 262168
  2.8 0.0 copy-start.2
  2.8 0.9 %copy-done.2 = bf16[4,256,128]{2,1,0:T(8,128)(2,1)S(1)} copy-done((bf16[4,256,128]{2,1,0:T(8,128)(2,1)S(1)}, bf16[4,256,128]{2,1,0:T(8,128)(2,1)}, u32[]{:S(2)}) %copy-start.2) | copy-done | bytes 262168
  3.8 74.4 %shard_map.50 = (f32[4,256,128]{2,1,0:T(8,128)S(1)}, f32[3,4,256,128]{3,2,1,0:T(8,128)S(1)}) custom-call(bf16[4,1024,128]{2,1,0:T(8,128)(2,1)S(1)} %bitcast.1, bf16[4,256,128]{2,1,0:T(8,128)(2,1)S(1)} %copy-done.1, bf16[4,256,128]{2,1,0:T(8,128)(2,1)S(1)} %copy-done.2), custom_call_target="tpu_custom_call" | custom-call | tf_op jit(solution)/shard_map/pallas_call | solution.py:223
  78.1 0.8 copy.7
  78.9 1.1 %copy.8 = f32[3,4,256,128]{3,2,1,0:T(8,128)} copy(f32[3,4,256,128]{3,2,1,0:T(8,128)S(1)} %get-tuple-element.5) | data formatting | bytes 3145728
Async XLA Ops:
  0.6 1.2 %copy-start = (bf16[4,128,8,128]{3,2,1,0:T(8,128)(2,1)S(1)}, bf16[4,128,8,128]{3,2,1,0:T(8,128)(2,1)}, u32[]{:S(2)}) copy-start(bf16[4,128,8,128]{3,2,1,0:T(8,128)(2,1)} %param.3) | copy-start | bytes 3145732
  1.9 0.9 %copy-start.1 = (bf16[4,256,128]{2,1,0:T(8,128)(2,1)S(1)}, bf16[4,256,128]{2,1,0:T(8,128)(2,1)}, u32[]{:S(2)}) copy-start(bf16[4,256,128]{2,1,0:T(8,128)(2,1)} %speed.1) | copy-start | bytes 786436
  2.8 0.9 %copy-start.2 = (bf16[4,256,128]{2,1,0:T(8,128)(2,1)S(1)}, bf16[4,256,128]{2,1,0:T(8,128)(2,1)}, u32[]{:S(2)}) copy-start(bf16[4,256,128]{2,1,0:T(8,128)(2,1)} %imp.1) | copy-start | bytes 786436

commit v2 on v1

v2 whole, which is shorter than its diff:
```python
import jax
import jax.numpy as jnp
from jax import lax
from jax.experimental import pallas as pl
from jax.experimental.pallas import tpu as pltpu
from jax.sharding import PartitionSpec as P

courant = 0.15
MESH = pl.DeviceIdType.MESH
SLABS = 32
F32 = jnp.float32
BF16 = jnp.bfloat16
PLAN = {'start': ((1, 1, 32),), 'sent0': ((2, 1, 32),), 'sent1': ((3, 1, 32),)}


def slab_device(slab, gy):
    return (slab // 16, lax.rem(slab, 16), gy)


def rounded(x):
    return x.astype(BF16).astype(F32)


def packed(layer_of):
    row = lax.broadcasted_iota(jnp.int32, (16, 128), 0)
    lane = lax.broadcasted_iota(jnp.int32, (16, 128), 1)
    total = None
    for j in range(8):
        pick = ((row == j) & (lane == 0)) | ((row == 8 + j) & (lane == 127))
        part = lax.dot_general(
            jnp.where(pick, 1.0, 0.0).astype(BF16),
            layer_of(j),
            (((1,), (1,)), ((), ())),
            preferred_element_type=F32,
        )
        total = part if total is None else total + part
    return total


def kernel(src, speed, imp, pres, vel, acc, sp, im, hs, sx, hx, zc, hc, zs, hz, stiff, buoy, vxm, fx, load, fy,
           total, edge, vzm, send, recv, own_sem, cs_send, cs_recv, cz_send, cz_recv, x_send, x_recv, z_send, z_recv):
    gy = lax.axis_index("gy")
    s = lax.axis_index("grp") * 16 + lax.axis_index("gx")
    above, below = lax.rem(s + 1, SLABS), lax.rem(s + SLABS - 1, SLABS)
    z_above, z_below = lax.rem(gy + 1, 8), lax.rem(gy + 7, 8)
    x_to = (slab_device(above, gy), slab_device(below, gy))
    z_to = (slab_device(s, z_above), slab_device(s, z_below))

    barrier = pltpu.get_barrier_semaphore()

    def greet(d, _):
        pl.semaphore_signal(barrier, inc=1, device_id=slab_device(lax.rem(s + d, SLABS), gy), device_id_type=MESH)
        return 0

    lax.fori_loop(1, SLABS, greet, 0)
    for to in z_to:
        pl.semaphore_signal(barrier, inc=1, device_id=to, device_id_type=MESH)

    own = pltpu.make_async_copy(src.at[:, pl.ds(32 * s, 32)], acc.at[:, pl.ds(32 * s, 32)], own_sem.at[0])
    own.start()
    fetch = (pltpu.make_async_copy(speed, sp, own_sem.at[1]), pltpu.make_async_copy(imp, im, own_sem.at[2]))
    for copy in fetch:
        copy.start()
    zero = jnp.zeros((256, 128), F32)

    def clear(l, _):
        for d in range(3):
            vel[d, l] = zero
        load[l, 256:264] = jnp.zeros((8, 128), F32)
        return 0

    lax.fori_loop(0, 4, clear, 0)
    vxm[...] = zero
    fy[0:8] = jnp.zeros((8, 128), F32)
    vzm[...] = jnp.zeros((8, 128), F32)
    for copy in fetch:
        copy.wait()

    def coefficients(l, _):
        a, b = sp[l].astype(F32), im[l].astype(F32)
        stiff[l + 1] = a * b
        buoy[l + 1] = a / b
        return 0

    lax.fori_loop(0, 4, coefficients, 0)

    packed_speed = packed(lambda j: sp[j // 2, 128 * (j % 2):128 * (j % 2) + 128])
    packed_imp = packed(lambda j: im[j // 2, 128 * (j % 2):128 * (j % 2) + 128])
    zc[0, 0:8] = packed_speed[8:16]
    zc[0, 8:16] = packed_imp[8:16]
    zc[1, 0:8] = packed_speed[0:8]
    zc[1, 8:16] = packed_imp[0:8]

    pl.semaphore_wait(barrier, SLABS - 1 + 2)

    def exchange(n, first, end):
        def one(d, _):
            to = lax.rem(s + d, SLABS)
            pltpu.make_async_remote_copy(
                src.at[3 - n, pl.ds(32 * to, 32)], acc.at[3 - n, pl.ds(32 * s, 32)], send, recv.at[n],
                device_id=slab_device(to, gy), device_id_type=MESH).start()
            return 0

        lax.fori_loop(first, end, one, 0)

    def exchanges(place):
        for part in PLAN.get(place, ()):
            exchange(*part)

    exchange(0, 1, SLABS)
    halo_x, halo_z = [], []
    for way in range(2):
        layer = 3 - 3 * way
        for k, field in enumerate((sp, im)):
            halo_x.append(pltpu.make_async_remote_copy(
                field.at[layer], hs.at[2 * way + k], cs_send.at[2 * way + k], cs_recv.at[2 * way + k],
                device_id=x_to[way], device_id_type=MESH))
        halo_z.append(pltpu.make_async_remote_copy(
            zc.at[way], hc.at[way], cz_send.at[way], cz_recv.at[way], device_id=z_to[way], device_id_type=MESH))
    for copy in halo_z + halo_x:
        copy.start()
    exchanges("start")
    own.wait()
    sent = halo_x + halo_z
    lane = lax.broadcasted_iota(jnp.int32, (256, 128), 1)
    has_below, has_above = jnp.where(s > 0, 1.0, 0.0), jnp.where(s < SLABS - 1, 1.0, 0.0)
    has_z_below, has_z_above = jnp.where(gy > 0, 1.0, 0.0), jnp.where(gy < 7, 1.0, 0.0)

    for n in range(4):
        pltpu.make_async_copy(acc.at[3 - n, 0:32 * 31], acc.at[3 - n, 0:32 * 31], recv.at[n]).wait()

        def add_source(i, _):
            x = acc[3 - n, pl.ds(pl.multiple_of(64 * i, 64), 64)].astype(F32).reshape(2, 4, 8, 128)
            rows = pl.ds(pl.multiple_of(16 * i, 16), 16)
            for l in range(4):
                now = x[:, l].reshape(16, 128)
                if n > 0:
                    now = pres[l, rows] + now
                pres[l, rows] = now
                if l in (0, 3):
                    sx[n, 0 if l == 3 else 1, rows] = now.astype(BF16)
            return 0

        lax.fori_loop(0, 16, add_source, 0, unroll=4)
        copies_x, copies_z = [], []
        for way in range(2):
            copies_x.append(pltpu.make_async_remote_copy(
                sx.at[n, way], hx.at[n, way], x_send.at[n, way], x_recv.at[n, way],
                device_id=x_to[way], device_id_type=MESH))
            copies_z.append(pltpu.make_async_remote_copy(
                zs.at[n, way], hz.at[n, way], z_send.at[n, way], z_recv.at[n, way],
                device_id=z_to[way], device_id_type=MESH))
        sent += copies_x + copies_z
        for copy in copies_x:
            copy.start()
        columns = packed(lambda j: pres[j // 2, 128 * (j % 2):128 * (j % 2) + 128].astype(BF16))
        zs[n, 0] = columns[8:16]
        zs[n, 1] = columns[0:8]
        for copy in copies_z:
            copy.start()
        exchanges(f"sent{n}")

        def inner(l, _):
            here = stiff[l + 1] * pres[l]
            load[l, 0:256] = here
            v1 = vel[1, l] + courant * (load[l, 1:257] - here)
            vel[1, l] = v1
            flux = buoy[l + 1] * v1
            fy[8:264] = flux
            total[l] = flux - fy[7:263]
            vel[2, l] = vel[2, l] + courant * (jnp.where(lane == 127, 0.0, pltpu.roll(here, 127, 1)) - here)
            return 0

        lax.fori_loop(0, 4, inner, 0)

        def inner_x(l, _):
            v = vel[0, l] + courant * (load[l + 1, 0:256] - load[l, 0:256])
            vel[0, l] = v
            flux = buoy[l + 1] * v
            fx[l] = flux
            return 0

        lax.fori_loop(0, 3, inner_x, 0)
        exchanges(f"inner{n}")

        if n == 0:
            for copy in halo_z:
                copy.wait_recv()
        for copy in copies_z:
            copy.wait_recv()
        past = hc[1, 0:8] * hc[1, 8:16] * hz[n, 1] * has_z_above
        before_v = vzm[...] + courant * (zc[1, 0:8] * zc[1, 8:16] * zs[n, 1] - hc[0, 0:8] * hc[0, 8:16] * hz[n, 0])
        vzm[...] = before_v
        before = hc[0, 0:8] / hc[0, 8:16] * before_v * has_z_below
        rows = jnp.concatenate(
            [rounded(past), past - rounded(past), rounded(before), before - rounded(before)], 0)
        columns = jnp.transpose(rows).astype(BF16)
        row32 = lax.broadcasted_iota(jnp.int32, (32, 128), 0)
        lane32 = lax.broadcasted_iota(jnp.int32, (32, 128), 1)
        for j in range(8):
            pick = (((row32 == j) | (row32 == 8 + j)) & (lane32 == 127)) | (
                ((row32 == 16 + j) | (row32 == 24 + j)) & (lane32 == 0))
            edge[j // 2, 128 * (j % 2):128 * (j % 2) + 128] = jnp.dot(
                columns, jnp.where(pick, 1.0, 0.0).astype(BF16), preferred_element_type=F32)

        def outer_z(l, _):
            rim = edge[l]
            v2 = vel[2, l] + courant * jnp.where(lane == 127, rim, 0.0)
            vel[2, l] = v2
            flux = buoy[l + 1] * v2
            total[l] = total[l] + (flux - jnp.where(lane == 0, rim, pltpu.roll(flux, 1, 1)))
            return 0

        lax.fori_loop(0, 4, outer_z, 0)

        def middle(l, _):
            pres[l] = pres[l] + courant * (total[l] + (fx[l] - fx[l - 1]))
            return 0

        lax.fori_loop(1, 3, middle, 0)
        exchanges(f"third{n}")

        if n == 0:
            for copy in halo_x:
                copy.wait_recv()
            stiff[0] = hs[0].astype(F32) * hs[1].astype(F32)
            buoy[0] = hs[0].astype(F32) / hs[1].astype(F32) * has_below
            stiff[5] = hs[2].astype(F32) * hs[3].astype(F32) * has_above
        for copy in copies_x:
            copy.wait_recv()
        v = vxm[...] + courant * (load[0, 0:256] - stiff[0] * hx[n, 0].astype(F32))
        vxm[...] = v
        pres[0] = pres[0] + courant * (total[0] + (fx[0] - buoy[0] * v))
        v = vel[0, 3] + courant * (stiff[5] * hx[n, 1].astype(F32) - load[3, 0:256])
        vel[0, 3] = v
        pres[3] = pres[3] + courant * (total[3] + (buoy[4] * v - fx[2]))

    for copy in sent:
        copy.wait_send()
    pltpu.make_async_copy(acc.at[:, 0:32 * 31], acc.at[:, 0:32 * 31], send).wait()


def on_device(source, speed, impedance):
    vmem = pl.BlockSpec(memory_space=pltpu.VMEM)
    hbm = pl.BlockSpec(memory_space=pltpu.HBM)
    dma = pltpu.SemaphoreType.DMA
    return pl.pallas_call(
        kernel,
        out_shape=(
            jax.ShapeDtypeStruct((4, 256, 128), F32),
            jax.ShapeDtypeStruct((3, 4, 256, 128), F32),
        ),
        in_specs=[hbm, hbm, hbm],
        out_specs=(vmem, vmem),
        scratch_shapes=[
            pltpu.VMEM((4, 1024, 128), BF16),
            pltpu.VMEM((4, 256, 128), BF16),
            pltpu.VMEM((4, 256, 128), BF16),
            pltpu.VMEM((4, 256, 128), BF16),
            pltpu.VMEM((4, 2, 256, 128), BF16),
            pltpu.VMEM((4, 2, 256, 128), BF16),
            pltpu.VMEM((2, 16, 128), F32),
            pltpu.VMEM((2, 16, 128), F32),
            pltpu.VMEM((4, 2, 8, 128), F32),
            pltpu.VMEM((4, 2, 8, 128), F32),
            pltpu.VMEM((6, 256, 128), F32),
            pltpu.VMEM((5, 256, 128), F32),
            pltpu.VMEM((256, 128), F32),
            pltpu.VMEM((3, 256, 128), F32),
            pltpu.VMEM((4, 264, 128), F32),
            pltpu.VMEM((264, 128), F32),
            pltpu.VMEM((4, 256, 128), F32),
            pltpu.VMEM((4, 256, 128), F32),
            pltpu.VMEM((8, 128), F32),
            dma, dma((4,)), dma((3,)), dma((4,)), dma((4,)), dma((2,)), dma((2,)),
            dma((4, 2)), dma((4, 2)), dma((4, 2)), dma((4, 2)),
        ],
        compiler_params=pltpu.CompilerParams(
            collective_id=0, has_side_effects=True, vmem_limit_bytes=48 * 1024 * 1024),
    )(source.reshape(4, 1024, 128), speed, impedance)


def solution(mesh):
    in_specs = (
        P(None, None, ("grp", "gx"), "gy"),
        P(("grp", "gx"), None, "gy"),
        P(("grp", "gx"), None, "gy"),
    )
    out_specs = (P(("grp", "gx"), None, "gy"), P(None, ("grp", "gx"), None, "gy"))
    return jax.shard_map(on_device, mesh=mesh, in_specs=in_specs, out_specs=out_specs, check_vma=False)
```

time: 80.3 us -> 63.8 us (0.79)
  Pallas kernels: 74.4 us -> 57.9 us
    pallas_call x1, Pallas kernels: 74.4 us -> 57.9 us  [on_device(): pl.pallas_call(kernel, out_shape=(jax.ShapeDtypeStruct((4, 256, 128), F32...]
where the time goes in v2:
time: 63.8 us; the launch traced here: 63.6 us
  Pallas kernels  57.9 us (91%)
  local copies, waits for them, and re-layouts  5.05 us (8%)
  between operations  0.65 us (1%)
    pallas_call x1, Pallas kernels, on_device(): pl.pallas_call(kernel, out_shape=(jax.ShapeDtypeStruct((4, 256, 128), F32...  57.9 us
    unnamed x8, local copies, waits for them, and re-layouts  5.05 us

profile of v2, /device:TPU:33, one launch (start us, length us, event | category | flops | bytes accessed | tf_op | source)
XLA Modules:
  0.0 63.6 jit_solution(11010939145781379062)
XLA Ops:
  0.6 0.0 copy-start
  0.6 1.2 %copy-done = bf16[4,128,8,128]{3,2,1,0:T(8,128)(2,1)S(1)} copy-done((bf16[4,128,8,128]{3,2,1,0:T(8,128)(2,1)S(1)}, bf16[4,128,8,128]{3,2,1,0:T(8,128)(2,1)}, u32[]{:S(2)}) %copy-start) | copy-done | bytes 1048600
  1.9 0.0 copy-start.1
  1.9 0.9 %copy-done.1 = bf16[4,256,128]{2,1,0:T(8,128)(2,1)S(1)} copy-done((bf16[4,256,128]{2,1,0:T(8,128)(2,1)S(1)}, bf16[4,256,128]{2,1,0:T(8,128)(2,1)}, u32[]{:S(2)}) %copy-start.1) | copy-done | bytes 262168
  2.8 0.0 copy-start.2
  2.8 0.9 %copy-done.2 = bf16[4,256,128]{2,1,0:T(8,128)(2,1)S(1)} copy-done((bf16[4,256,128]{2,1,0:T(8,128)(2,1)S(1)}, bf16[4,256,128]{2,1,0:T(8,128)(2,1)}, u32[]{:S(2)}) %copy-start.2) | copy-done | bytes 262168
  3.8 57.9 %shard_map.50 = (f32[4,256,128]{2,1,0:T(8,128)S(1)}, f32[3,4,256,128]{3,2,1,0:T(8,128)S(1)}) custom-call(bf16[4,1024,128]{2,1,0:T(8,128)(2,1)S(1)} %bitcast.1, bf16[4,256,128]{2,1,0:T(8,128)(2,1)S(1)} %copy-done.1, bf16[4,256,128]{2,1,0:T(8,128)(2,1)S(1)} %copy-done.2), custom_call_target="tpu_custom_call" | custom-call | tf_op jit(solution)/shard_map/pallas_call | solution.py:247
  61.7 0.8 %copy.7 = f32[4,256,128]{2,1,0:T(8,128)} copy(f32[4,256,128]{2,1,0:T(8,128)S(1)} %get-tuple-element.4) | data formatting | bytes 1048576
  62.5 1.1 %copy.8 = f32[3,4,256,128]{3,2,1,0:T(8,128)} copy(f32[3,4,256,128]{3,2,1,0:T(8,128)S(1)} %get-tuple-element.5) | data formatting | bytes 3145728
Async XLA Ops:
  0.6 1.2 %copy-start = (bf16[4,128,8,128]{3,2,1,0:T(8,128)(2,1)S(1)}, bf16[4,128,8,128]{3,2,1,0:T(8,128)(2,1)}, u32[]{:S(2)}) copy-start(bf16[4,128,8,128]{3,2,1,0:T(8,128)(2,1)} %param.3) | copy-start | bytes 3145732
  1.9 0.9 %copy-start.1 = (bf16[4,256,128]{2,1,0:T(8,128)(2,1)S(1)}, bf16[4,256,128]{2,1,0:T(8,128)(2,1)}, u32[]{:S(2)}) copy-start(bf16[4,256,128]{2,1,0:T(8,128)(2,1)} %speed.1) | copy-start | bytes 786436
  2.8 0.9 %copy-start.2 = (bf16[4,256,128]{2,1,0:T(8,128)(2,1)S(1)}, bf16[4,256,128]{2,1,0:T(8,128)(2,1)}, u32[]{:S(2)}) copy-start(bf16[4,256,128]{2,1,0:T(8,128)(2,1)} %imp.1) | copy-start | bytes 786436

commit v3 on v2

--- a/solution.py
+++ b/solution.py
@@ -10,6 +10,7 @@
 SLABS = 32
 F32 = jnp.float32
 BF16 = jnp.bfloat16
+STRIDE = 1
 PLAN = {'start': ((1, 1, 32),), 'sent0': ((2, 1, 32),), 'sent1': ((3, 1, 32),)}
 
 
@@ -78,24 +79,23 @@
 
     def coefficients(l, _):
         a, b = sp[l].astype(F32), im[l].astype(F32)
-        stiff[l + 1] = a * b
+        stiff[l] = a * b
         buoy[l + 1] = a / b
         return 0
 
     lax.fori_loop(0, 4, coefficients, 0)
+    hs[0] = buoy[4].astype(BF16)
 
     packed_speed = packed(lambda j: sp[j // 2, 128 * (j % 2):128 * (j % 2) + 128])
     packed_imp = packed(lambda j: im[j // 2, 128 * (j % 2):128 * (j % 2) + 128])
-    zc[0, 0:8] = packed_speed[8:16]
-    zc[0, 8:16] = packed_imp[8:16]
-    zc[1, 0:8] = packed_speed[0:8]
-    zc[1, 8:16] = packed_imp[0:8]
+    zc[0:8] = packed_speed[8:16]
+    zc[8:16] = packed_imp[8:16]
 
     pl.semaphore_wait(barrier, SLABS - 1 + 2)
 
     def exchange(n, first, end):
         def one(d, _):
-            to = lax.rem(s + d, SLABS)
+            to = lax.rem(s + 1 + lax.rem((d - 1) * STRIDE, SLABS - 1), SLABS)
             pltpu.make_async_remote_copy(
                 src.at[3 - n, pl.ds(32 * to, 32)], acc.at[3 - n, pl.ds(32 * s, 32)], send, recv.at[n],
                 device_id=slab_device(to, gy), device_id_type=MESH).start()
@@ -109,17 +109,14 @@
 
     exchange(0, 1, SLABS)
     halo_x, halo_z = [], []
-    for way in range(2):
-        layer = 3 - 3 * way
-        for k, field in enumerate((sp, im)):
-            halo_x.append(pltpu.make_async_remote_copy(
-                field.at[layer], hs.at[2 * way + k], cs_send.at[2 * way + k], cs_recv.at[2 * way + k],
-                device_id=x_to[way], device_id_type=MESH))
-        halo_z.append(pltpu.make_async_remote_copy(
-            zc.at[way], hc.at[way], cz_send.at[way], cz_recv.at[way], device_id=z_to[way], device_id_type=MESH))
-    for copy in halo_z + halo_x:
+    halo_z.append(pltpu.make_async_remote_copy(zc, hc, cz_send, cz_recv, device_id=z_to[0], device_id_type=MESH))
+    halo_x.append(pltpu.make_async_remote_copy(
+        hs.at[0], hs.at[1], cs_send, cs_recv, device_id=x_to[0], device_id_type=MESH))
+    for copy in halo_z:
         copy.start()
     exchanges("start")
+    for copy in halo_x:
+        copy.start()
     own.wait()
     sent = halo_x + halo_z
     lane = lax.broadcasted_iota(jnp.int32, (256, 128), 1)
@@ -137,6 +134,8 @@
                 if n > 0:
                     now = pres[l, rows] + now
                 pres[l, rows] = now
+                now = stiff[l, rows] * now
+                load[l, rows] = now
                 if l in (0, 3):
                     sx[n, 0 if l == 3 else 1, rows] = now.astype(BF16)
             return 0
@@ -151,18 +150,15 @@
                 zs.at[n, way], hz.at[n, way], z_send.at[n, way], z_recv.at[n, way],
                 device_id=z_to[way], device_id_type=MESH))
         sent += copies_x + copies_z
-        for copy in copies_x:
-            copy.start()
-        columns = packed(lambda j: pres[j // 2, 128 * (j % 2):128 * (j % 2) + 128].astype(BF16))
+        columns = packed(lambda j: load[j // 2, 128 * (j % 2):128 * (j % 2) + 128].astype(BF16))
         zs[n, 0] = columns[8:16]
         zs[n, 1] = columns[0:8]
-        for copy in copies_z:
+        for copy in copies_z + copies_x:
             copy.start()
         exchanges(f"sent{n}")
 
         def inner(l, _):
-            here = stiff[l + 1] * pres[l]
-            load[l, 0:256] = here
+            here = load[l, 0:256]
             v1 = vel[1, l] + courant * (load[l, 1:257] - here)
             vel[1, l] = v1
             flux = buoy[l + 1] * v1
@@ -188,10 +184,10 @@
                 copy.wait_recv()
         for copy in copies_z:
             copy.wait_recv()
-        past = hc[1, 0:8] * hc[1, 8:16] * hz[n, 1] * has_z_above
-        before_v = vzm[...] + courant * (zc[1, 0:8] * zc[1, 8:16] * zs[n, 1] - hc[0, 0:8] * hc[0, 8:16] * hz[n, 0])
+        past = hz[n, 1] * has_z_above
+        before_v = vzm[...] + courant * (zs[n, 1] - hz[n, 0])
         vzm[...] = before_v
-        before = hc[0, 0:8] / hc[0, 8:16] * before_v * has_z_below
+        before = hc[0:8] / hc[8:16] * before_v * has_z_below
         rows = jnp.concatenate(
             [rounded(past), past - rounded(past), rounded(before), before - rounded(before)], 0)
         columns = jnp.transpose(rows).astype(BF16)
@@ -223,15 +219,13 @@
         if n == 0:
             for copy in halo_x:
                 copy.wait_recv()
-            stiff[0] = hs[0].astype(F32) * hs[1].astype(F32)
-            buoy[0] = hs[0].astype(F32) / hs[1].astype(F32) * has_below
-            stiff[5] = hs[2].astype(F32) * hs[3].astype(F32) * has_above
+            buoy[0] = hs[1].astype(F32) * has_below
         for copy in copies_x:
             copy.wait_recv()
-        v = vxm[...] + courant * (load[0, 0:256] - stiff[0] * hx[n, 0].astype(F32))
+        v = vxm[...] + courant * (load[0, 0:256] - hx[n, 0].astype(F32))
         vxm[...] = v
         pres[0] = pres[0] + courant * (total[0] + (fx[0] - buoy[0] * v))
-        v = vel[0, 3] + courant * (stiff[5] * hx[n, 1].astype(F32) - load[3, 0:256])
+        v = vel[0, 3] + courant * (hx[n, 1].astype(F32) * has_above - load[3, 0:256])
         vel[0, 3] = v
         pres[3] = pres[3] + courant * (total[3] + (buoy[4] * v - fx[2]))
 
@@ -256,14 +250,14 @@
             pltpu.VMEM((4, 1024, 128), BF16),
             pltpu.VMEM((4, 256, 128), BF16),
             pltpu.VMEM((4, 256, 128), BF16),
-            pltpu.VMEM((4, 256, 128), BF16),
+            pltpu.VMEM((2, 256, 128), BF16),
             pltpu.VMEM((4, 2, 256, 128), BF16),
             pltpu.VMEM((4, 2, 256, 128), BF16),
-            pltpu.VMEM((2, 16, 128), F32),
-            pltpu.VMEM((2, 16, 128), F32),
+            pltpu.VMEM((16, 128), F32),
+            pltpu.VMEM((16, 128), F32),
             pltpu.VMEM((4, 2, 8, 128), F32),
             pltpu.VMEM((4, 2, 8, 128), F32),
-            pltpu.VMEM((6, 256, 128), F32),
+            pltpu.VMEM((4, 256, 128), F32),
             pltpu.VMEM((5, 256, 128), F32),
             pltpu.VMEM((256, 128), F32),
             pltpu.VMEM((3, 256, 128), F32),
@@ -272,12 +266,12 @@
             pltpu.VMEM((4, 256, 128), F32),
             pltpu.VMEM((4, 256, 128), F32),
             pltpu.VMEM((8, 128), F32),
-            dma, dma((4,)), dma((3,)), dma((4,)), dma((4,)), dma((2,)), dma((2,)),
+            dma, dma((4,)), dma((3,)), dma, dma, dma, dma,
             dma((4, 2)), dma((4, 2)), dma((4, 2)), dma((4, 2)),
         ],
         compiler_params=pltpu.CompilerParams(
             collective_id=0, has_side_effects=True, vmem_limit_bytes=48 * 1024 * 1024),
-    )(source.reshape(4, 1024, 128), speed, impedance)
+    )(*(pltpu.with_memory_space_constraint(a, pltpu.HBM) for a in (source.reshape(4, 1024, 128), speed, impedance)))
 
 
 def solution(mesh):

time: 63.8 us -> 58.3 us (0.914)
  the two profiles are of different devices: /device:TPU:33 before, /device:TPU:1 now
where the time goes in v3:
time: 58.3 us; the launch traced here: 58.2 us
  Pallas kernels  55.6 us (95%)
  local copies, waits for them, and re-layouts  1.94 us (3%)
  between operations  0.64 us (1%)
    pallas_call x1, Pallas kernels, on_device(): pl.pallas_call(kernel, out_shape=(jax.ShapeDtypeStruct((4, 256, 128), F32...  55.6 us
    unnamed x2, local copies, waits for them, and re-layouts  1.94 us

profile of v3, /device:TPU:1, one launch (start us, length us, event | category | flops | bytes accessed | tf_op | source)
XLA Modules:
  0.0 58.2 jit_solution(8422357265063349064)
XLA Ops:
  0.6 55.6 %shard_map.50 = (f32[4,256,128]{2,1,0:T(8,128)S(1)}, f32[3,4,256,128]{3,2,1,0:T(8,128)S(1)}) custom-call(bf16[4,1024,128]{2,1,0:T(8,128)(2,1)} %bitcast.1, bf16[4,256,128]{2,1,0:T(8,128)(2,1)} %speed.1, bf16[4,256,128]{2,1,0:T(8,128)(2,1)} %imp.1), custom_call_target="tpu_custom_call" | custom-call | tf_op jit(solution)/shard_map/pallas_call | solution.py:241
  56.2 0.8 %copy.7 = f32[4,256,128]{2,1,0:T(8,128)} copy(f32[4,256,128]{2,1,0:T(8,128)S(1)} %get-tuple-element.4) | data formatting | bytes 1048576
  57.0 1.1 %copy.8 = f32[3,4,256,128]{3,2,1,0:T(8,128)} copy(f32[3,4,256,128]{3,2,1,0:T(8,128)S(1)} %get-tuple-element.5) | data formatting | bytes 3145728

commit v4 on v3

v4 whole, which is shorter than its diff:
```python
import jax
import jax.numpy as jnp
from jax import lax
from jax.experimental import pallas as pl
from jax.experimental.pallas import tpu as pltpu
from jax.sharding import PartitionSpec as P

courant = 0.15
MESH = pl.DeviceIdType.MESH
SLABS = 32
F32 = jnp.float32
BF16 = jnp.bfloat16
STRIDE = 1
PLAN = {'half0': ((1, 1, 32),), 'sent0': ((2, 1, 32),), 'sent1': ((3, 1, 32),)}


def slab_device(slab, gy):
    return (slab // 16, lax.rem(slab, 16), gy)


def rounded(x):
    return x.astype(BF16).astype(F32)


def packed(layer_of, blocks=range(8)):
    row = lax.broadcasted_iota(jnp.int32, (16, 128), 0)
    lane = lax.broadcasted_iota(jnp.int32, (16, 128), 1)
    total = None
    for j in blocks:
        pick = ((row == j) & (lane == 0)) | ((row == 8 + j) & (lane == 127))
        part = lax.dot_general(
            jnp.where(pick, 1.0, 0.0).astype(BF16),
            layer_of(j),
            (((1,), (1,)), ((), ())),
            preferred_element_type=F32,
        )
        total = part if total is None else total + part
    return total


def kernel(src, speed, imp, pres, vel, acc, sp, im, hs, sx, hx, zc, hc, zs, hz, stiff, buoy, vxm, fx, load, fy,
           total, edge, vzm, owed, shares, zo, send, recv, own_sem, cs_send, cs_recv, cz_send, cz_recv, x_send, x_recv, z_send, z_recv):
    gy = lax.axis_index("gy")
    s = lax.axis_index("grp") * 16 + lax.axis_index("gx")
    above, below = lax.rem(s + 1, SLABS), lax.rem(s + SLABS - 1, SLABS)
    z_above, z_below = lax.rem(gy + 1, 8), lax.rem(gy + 7, 8)
    x_to = (slab_device(above, gy), slab_device(below, gy))
    z_to = (slab_device(s, z_above), slab_device(s, z_below))

    barrier = pltpu.get_barrier_semaphore()

    def greet(d, _):
        pl.semaphore_signal(barrier, inc=1, device_id=slab_device(lax.rem(s + d, SLABS), gy), device_id_type=MESH)
        return 0

    lax.fori_loop(1, SLABS, greet, 0)
    for to in z_to:
        pl.semaphore_signal(barrier, inc=1, device_id=to, device_id_type=MESH)

    own = pltpu.make_async_copy(src.at[:, pl.ds(32 * s, 32)], acc.at[:, pl.ds(32 * s, 32)], own_sem.at[0])
    own.start()
    fetch = (pltpu.make_async_copy(speed, sp, own_sem.at[1]), pltpu.make_async_copy(imp, im, own_sem.at[2]))
    for copy in fetch:
        copy.start()
    zero = jnp.zeros((256, 128), F32)

    def clear(l, _):
        for d in range(3):
            vel[d, l] = zero
        load[l, 256:264] = jnp.zeros((8, 128), F32)
        return 0

    lax.fori_loop(0, 4, clear, 0)
    vxm[...] = zero
    fy[0:8] = jnp.zeros((8, 128), F32)
    vzm[...] = jnp.zeros((8, 128), F32)
    for copy in fetch:
        copy.wait()

    def coefficients(l, _):
        a, b = sp[l].astype(F32), im[l].astype(F32)
        stiff[l] = a * b
        buoy[l + 1] = a / b
        return 0

    lax.fori_loop(0, 4, coefficients, 0)
    hs[0] = buoy[4].astype(BF16)

    packed_speed = packed(lambda j: sp[j // 2, 128 * (j % 2):128 * (j % 2) + 128])
    packed_imp = packed(lambda j: im[j // 2, 128 * (j % 2):128 * (j % 2) + 128])
    zo[0:16] = packed_speed
    zo[16:32] = packed_imp
    zc[0:8] = packed_speed[8:16]
    zc[8:16] = packed_imp[8:16]

    pl.semaphore_wait(barrier, SLABS - 1 + 2)

    def exchange_half(n, first, end, half):
        def one(d, _):
            to = lax.rem(s + 1 + lax.rem((d - 1) * STRIDE, SLABS - 1), SLABS)
            pltpu.make_async_remote_copy(
                src.at[3 - n, pl.ds(32 * to, 32)], acc.at[3 - n, pl.ds(32 * s, 32)], send, recv.at[n, half],
                device_id=slab_device(to, gy), device_id_type=MESH).start()
            return 0

        lax.fori_loop(first, end, one, 0)

    def exchange(n, first, end):
        if first < 16:
            exchange_half(n, first, min(end, 16), 0)
        if end > 16:
            exchange_half(n, max(first, 16), end, 1)

    def exchanges(place):
        for part in PLAN.get(place, ()):
            exchange(*part)

    halo_x = [pltpu.make_async_remote_copy(
        hs.at[0], hs.at[1], cs_send, cs_recv, device_id=x_to[0], device_id_type=MESH)]
    halo_z = [pltpu.make_async_remote_copy(zc, hc, cz_send, cz_recv, device_id=z_to[0], device_id_type=MESH)]
    for copy in halo_z + halo_x:
        copy.start()
    exchange(0, 1, SLABS)
    exchanges("start")
    own.wait()
    sent = halo_x + halo_z
    lane = lax.broadcasted_iota(jnp.int32, (256, 128), 1)
    has_below, has_above = jnp.where(s > 0, 1.0, 0.0), jnp.where(s < SLABS - 1, 1.0, 0.0)
    has_z_below, has_z_above = jnp.where(gy > 0, 1.0, 0.0), jnp.where(gy < 7, 1.0, 0.0)

    def add_source(n):
        for half in range(2):
            blocks = acc.at[3 - n, 0:32 * (15 + half)]
            pltpu.make_async_copy(blocks, blocks, recv.at[n, half]).wait()
            if half == 0:
                exchanges(f"half{n}")

        def one(i, _):
            x = acc[3 - n, pl.ds(pl.multiple_of(64 * i, 64), 64)].astype(F32).reshape(2, 4, 8, 128)
            rows = pl.ds(pl.multiple_of(16 * i, 16), 16)
            for l in range(4):
                now = x[:, l].reshape(16, 128)
                if n > 0:
                    now = pres[l, rows] + now
                pres[l, rows] = now
                now = stiff[l, rows] * now
                load[l, rows] = now
                if n == 0 and l in (0, 3):
                    sx[n, 0 if l == 3 else 1, rows] = now.astype(BF16)
            return 0

        lax.fori_loop(0, 16, one, 0, unroll=4)

    def send_halos(n, buffers, sems, to):
        copies = [
            pltpu.make_async_remote_copy(
                buffers[0].at[n, way], buffers[1].at[n, way], sems[0].at[n, way], sems[1].at[n, way],
                device_id=to[way], device_id_type=MESH)
            for way in range(2)]
        sent.extend(copies)
        for copy in copies:
            copy.start()
        return copies

    def load_part(j):
        return load[j // 2, 128 * (j % 2):128 * (j % 2) + 128].astype(BF16)

    def owed_part(j):
        return owed[j // 6, 128 * (j % 2):128 * (j % 2) + 128]

    row32 = lax.broadcasted_iota(jnp.int32, (32, 128), 0)
    lane32 = lax.broadcasted_iota(jnp.int32, (32, 128), 1)

    def spread(columns, j):
        pick = (((row32 == j) | (row32 == 8 + j)) & (lane32 == 127)) | (
            ((row32 == 16 + j) | (row32 == 24 + j)) & (lane32 == 0))
        edge[j // 2, 128 * (j % 2):128 * (j % 2) + 128] = jnp.dot(
            columns, jnp.where(pick, 1.0, 0.0).astype(BF16), preferred_element_type=F32)

    def rim_share(l):
        rim = edge[l]
        dv = courant * jnp.where(lane == 127, rim, 0.0)
        vel[2, l] = vel[2, l] + dv
        return courant * (buoy[l + 1] * dv - jnp.where(lane == 0, rim, 0.0))

    add_source(0)
    copies_x = send_halos(0, (sx, hx), (x_send, x_recv), x_to)
    columns = packed(load_part)
    zs[0, 0] = columns[8:16]
    zs[0, 1] = columns[0:8]
    copies_z = send_halos(0, (zs, hz), (z_send, z_recv), z_to)
    for n in range(4):
        exchanges(f"sent{n}")

        def inner(l, _):
            here = load[l, 0:256]
            v1 = vel[1, l] + courant * (load[l, 1:257] - here)
            vel[1, l] = v1
            flux = buoy[l + 1] * v1
            fy[8:264] = flux
            part = flux - fy[7:263]
            v2 = vel[2, l] + courant * (jnp.where(lane == 127, 0.0, pltpu.roll(here, 127, 1)) - here)
            vel[2, l] = v2
            flux = buoy[l + 1] * v2
            total[l] = part + (flux - jnp.where(lane == 0, 0.0, pltpu.roll(flux, 1, 1)))
            return 0

        lax.fori_loop(0, 4, inner, 0)

        def inner_x(l, _):
            v = vel[0, l] + courant * (load[l + 1, 0:256] - load[l, 0:256])
            vel[0, l] = v
            fx[l] = buoy[l + 1] * v
            return 0

        lax.fori_loop(0, 3, inner_x, 0)
        if n == 0:
            for copy in halo_x:
                copy.wait_recv()
            buoy[0] = hs[1].astype(F32) * has_below
        v = vxm[...] + courant * load[0, 0:256]
        vxm[...] = v
        pres[0] = pres[0] + courant * (total[0] + (fx[0] - buoy[0] * v))
        v = vel[0, 3] - courant * load[3, 0:256]
        vel[0, 3] = v
        pres[3] = pres[3] + courant * (total[3] + (buoy[4] * v - fx[2]))

        def middle(l, _):
            pres[l] = pres[l] + courant * (total[l] + (fx[l] - fx[l - 1]))
            return 0

        lax.fori_loop(1, 3, middle, 0)
        if n < 3:
            add_source(n + 1)
            ready = packed(load_part)
        exchanges(f"inner{n}")

        if n == 0:
            for copy in halo_z:
                copy.wait_recv()
        for copy in copies_z:
            copy.wait_recv()
        exchanges(f"third{n}")
        past = hz[n, 1] * has_z_above
        before_v = vzm[...] + courant * (zs[n, 1] - hz[n, 0])
        vzm[...] = before_v
        before = hc[0:8] / hc[8:16] * before_v * has_z_below
        rows = jnp.concatenate(
            [rounded(past), past - rounded(past), rounded(before), before - rounded(before)], 0)
        columns = jnp.transpose(rows).astype(BF16)
        for j in (0, 1, 6, 7):
            spread(columns, j)
        for k, l in enumerate((0, 3)):
            shares[k] = rim_share(l)

        for copy in copies_x:
            copy.wait_recv()
        below_x = hx[n, 0].astype(F32)
        vxm[...] = vxm[...] - courant * below_x
        share_0 = courant * courant * buoy[0] * below_x
        dv = courant * has_above * hx[n, 1].astype(F32)
        vel[0, 3] = vel[0, 3] + dv
        share_3 = courant * buoy[4] * dv
        for k, (l, share) in enumerate(((0, share_0), (3, share_3))):
            whole = shares[k] + share
            pres[l] = pres[l] + whole
            if n < 3:
                owed[k] = (stiff[l] * share).astype(BF16)
                now = load[l, 0:256] + stiff[l] * whole
                load[l, 0:256] = now
                sx[n + 1, 1 - k] = now.astype(BF16)
        if n < 3:
            copies_x = send_halos(n + 1, (sx, hx), (x_send, x_recv), x_to)
            ready = ready + packed(owed_part, (0, 1, 6, 7))
            zs[n + 1, 0] = ready[8:16] + courant * courant * zo[8:16] * zo[8:16] * past
            zs[n + 1, 1] = ready[0:8] - courant * zo[0:8] * zo[16:24] * before
            copies_z = send_halos(n + 1, (zs, hz), (z_send, z_recv), z_to)
        for j in (2, 3, 4, 5):
            spread(columns, j)

        def rest(l, _):
            share = rim_share(l)
            pres[l] = pres[l] + share
            if n < 3:
                load[l, 0:256] = load[l, 0:256] + stiff[l] * share
            return 0

        lax.fori_loop(1, 3, rest, 0)

    for copy in sent:
        copy.wait_send()
    pltpu.make_async_copy(acc.at[:, 0:32 * 31], acc.at[:, 0:32 * 31], send).wait()


def flush(pres, vel, pres_out, vel_out, sem):
    copies = [pltpu.make_async_copy(vel.at[d], vel_out.at[d], sem.at[d]) for d in range(3)]
    copies.append(pltpu.make_async_copy(pres, pres_out, sem.at[3]))
    for copy in copies:
        copy.start()
    for copy in copies:
        copy.wait()


def on_device(source, speed, impedance):
    vmem = pl.BlockSpec(memory_space=pltpu.VMEM)
    hbm = pl.BlockSpec(memory_space=pltpu.HBM)
    dma = pltpu.SemaphoreType.DMA
    held = pl.pallas_call(
        kernel,
        out_shape=(
            jax.ShapeDtypeStruct((4, 256, 128), F32),
            jax.ShapeDtypeStruct((3, 4, 256, 128), F32),
        ),
        in_specs=[hbm, hbm, hbm],
        out_specs=(vmem, vmem),
        scratch_shapes=[
            pltpu.VMEM((4, 1024, 128), BF16),
            pltpu.VMEM((4, 256, 128), BF16),
            pltpu.VMEM((4, 256, 128), BF16),
            pltpu.VMEM((2, 256, 128), BF16),
            pltpu.VMEM((4, 2, 256, 128), BF16),
            pltpu.VMEM((4, 2, 256, 128), BF16),
            pltpu.VMEM((16, 128), F32),
            pltpu.VMEM((16, 128), F32),
            pltpu.VMEM((4, 2, 8, 128), F32),
            pltpu.VMEM((4, 2, 8, 128), F32),
            pltpu.VMEM((4, 256, 128), F32),
            pltpu.VMEM((5, 256, 128), F32),
            pltpu.VMEM((256, 128), F32),
            pltpu.VMEM((3, 256, 128), F32),
            pltpu.VMEM((4, 264, 128), F32),
            pltpu.VMEM((264, 128), F32),
            pltpu.VMEM((4, 256, 128), F32),
            pltpu.VMEM((4, 256, 128), F32),
            pltpu.VMEM((8, 128), F32),
            pltpu.VMEM((2, 256, 128), BF16),
            pltpu.VMEM((2, 256, 128), F32),
            pltpu.VMEM((32, 128), F32),
            dma, dma((4, 2)), dma((3,)), dma, dma, dma, dma,
            dma((4, 2)), dma((4, 2)), dma((4, 2)), dma((4, 2)),
        ],
        compiler_params=pltpu.CompilerParams(
            collective_id=0, has_side_effects=True, vmem_limit_bytes=48 * 1024 * 1024),
    )(*(pltpu.with_memory_space_constraint(a, pltpu.HBM) for a in (source.reshape(4, 1024, 128), speed, impedance)))
    return pl.pallas_call(
        flush,
        out_shape=(
            jax.ShapeDtypeStruct((4, 256, 128), F32),
            jax.ShapeDtypeStruct((3, 4, 256, 128), F32),
        ),
        in_specs=[vmem, vmem],
        out_specs=(hbm, hbm),
        scratch_shapes=[dma((4,))],
        compiler_params=pltpu.CompilerParams(vmem_limit_bytes=8 * 1024 * 1024),
    )(*held)


def solution(mesh):
    in_specs = (
        P(None, None, ("grp", "gx"), "gy"),
        P(("grp", "gx"), None, "gy"),
        P(("grp", "gx"), None, "gy"),
    )
    out_specs = (P(("grp", "gx"), None, "gy"), P(None, ("grp", "gx"), None, "gy"))
    return jax.shard_map(on_device, mesh=mesh, in_specs=in_specs, out_specs=out_specs, check_vma=False)
```

time: 58.3 us -> 57 us (0.978)
  local copies, waits for them, and re-layouts: 1.94 us -> 0 us
  Pallas kernels: 55.6 us -> 56.3 us
    unnamed x2 -> x0, local copies, waits for them, and re-layouts: 1.94 us -> none
    pallas_call x0 -> x1, Pallas kernels: none -> 1.35 us  [on_device(): pl.pallas_call(flush, out_shape=(jax.ShapeDtypeStruct((4, 256, 128), F32)...]
    pallas_call x1, Pallas kernels: 55.6 us -> 55 us  [on_device(): pl.pallas_call(kernel, out_shape=(jax.ShapeDtypeStruct((4, 256, 128), F32...]
where the time goes in v4:
time: 57 us; the launch traced here: 56.9 us
  Pallas kernels  56.3 us (99%)
  between operations  0.64 us (1%)
    pallas_call x1, Pallas kernels, on_device(): pl.pallas_call(kernel, out_shape=(jax.ShapeDtypeStruct((4, 256, 128), F32...  55 us
    pallas_call x1, Pallas kernels, on_device(): pl.pallas_call(flush, out_shape=(jax.ShapeDtypeStruct((4, 256, 128), F32)...  1.35 us

profile of v4, /device:TPU:1, one launch (start us, length us, event | category | flops | bytes accessed | tf_op | source)
XLA Modules:
  0.0 56.9 jit_solution(9471998160150226847)
XLA Ops:
  0.6 55.0 %shard_map.50 = (f32[4,256,128]{2,1,0:T(8,128)S(1)}, f32[3,4,256,128]{3,2,1,0:T(8,128)S(1)}) custom-call(bf16[4,1024,128]{2,1,0:T(8,128)(2,1)} %bitcast.1, bf16[4,256,128]{2,1,0:T(8,128)(2,1)} %speed.1, bf16[4,256,128]{2,1,0:T(8,128)(2,1)} %imp.1), custom_call_target="tpu_custom_call" | custom-call | tf_op jit(solution)/shard_map/pallas_call | solution.py:308
  55.6 1.3 %shard_map.51 = (f32[4,256,128]{2,1,0:T(8,128)}, f32[3,4,256,128]{3,2,1,0:T(8,128)}) custom-call(f32[4,256,128]{2,1,0:T(8,128)S(1)} %get-tuple-element.4.pres, f32[3,4,256,128]{3,2,1,0:T(8,128)S(1)} %get-tuple-element.5.vel), custom_call_target="tpu_custom_call" | custom-call | tf_op jit(solution)/shard_map/pallas_call | solution.py:345
